TPU v7x, 32 devices: a whole 2x2x4 slice. The times are simulated.
32 devices in a mesh: occ: 4 (over y, x), vir: 8 (over z, core).
Axes of the slice: x: 2, y: 2, z: 4, core: 2. Of those that a mesh axis runs over, the one named last changes fastest.
Arguments:
- amplitudes: bfloat16 [32, 32, 589824], P(None, None, ('occ', 'vir')), may hold values from -6 to 6
- ladder_integrals: bfloat16 [32, 32, 589824], P(None, None, ('occ', 'vir')), may hold values from -0.015625 to 0.015625
- driver: float32 [32, 32, 1024], P('occ', 'vir'), may hold values from -6 to 6
- occ_energy: float32 [32], replicated, may hold values from -2 to -0.5
- vir_energy: float32 [32], replicated, may hold values from 0.5 to 4
- occ_irrep: int32 [32], replicated, may hold values from 0 to 3
- vir_tile_irrep: int32 [12], replicated, may hold values from 0 to 3
Outputs:
- updated: float32 [32, 32, 1024], P('occ', 'vir')
All inputs are finite; a program needn't handle non-finite values.
Results may differ from a plain program's by a relative error of at most 0.0003.
Values sent between devices are 32-bit elements; how exact they have to be, the bound alone decides.
No kernel may reach another device: no remote copies, remote signals or barrier semaphores. Data moves between devices by JAX's collectives and lax.ppermute only.
A program may use at most 192 MiB of HBM per device.

v0:
```python
import functools
import math

import jax
import jax.numpy as jnp
from jax import lax
from jax.experimental import pallas as pl
from jax.experimental.pallas import tpu as pltpu
from jax.sharding import PartitionSpec as P

NV = 768
TILE = 64
LANES = 128
IRREPS = 4
SIZES = (10, 12)
CHUNK = 16


def ladder_kernel(occ_irrep, vir_irrep, place, ycode_ref, t_hbm, v_hbm, *refs, cs, occ_local, steps):
    out_refs = refs[:4]
    t_buf, v_buf, acc, tp_even, tp_odd, zs, xs, codes, table, slot_of, count, sems = refs[4:]
    occupied = t_hbm.shape[0]
    virtual = v_hbm.shape[0]
    groups = NV // LANES
    tiles = virtual * virtual // LANES
    per_tile = LANES // virtual
    lane = lax.broadcasted_iota(jnp.int32, (occupied, LANES), 1)
    band = 2 * LANES // virtual

    total = steps * groups

    def copies(which, step):
        src, dst = ((t_hbm, t_buf), (v_hbm, v_buf))[which]
        made = []
        for c in range(cs):
            start = pl.multiple_of((step // groups * cs + c) * NV + step % groups * LANES, LANES)
            made.append(pltpu.make_async_copy(
                src.at[:, :, pl.ds(start, LANES)], dst.at[step % 2, c], sems.at[step % 2, which, c]
            ))
        return made

    def start_all(which, step):
        for copy in copies(which, step):
            copy.start()

    def wait_all(which, step):
        for copy in copies(which, step):
            copy.wait()

    start_all(0, 0)
    start_all(1, 0)
    start_all(0, 1)

    for x in range(IRREPS):
        count[x] = 0

    @pl.loop(0, table.shape[0])
    def _(s):
        table[s] = 0

    @pl.loop(0, occupied)
    def _(i):
        x = occ_irrep[i]
        s = count[x]
        table[s * IRREPS + x] = i
        slot_of[i] = s
        count[x] = s + 1

    most = jnp.maximum(jnp.maximum(count[0], count[1]), jnp.maximum(count[2], count[3]))
    count[IRREPS] = most
    for label in range(IRREPS):
        codes[label] = jnp.bitwise_xor(ycode_ref[...], label).astype(jnp.float32).astype(jnp.bfloat16)
    codes[IRREPS] = (lane // (LANES // 2)).astype(jnp.float32).astype(jnp.bfloat16)

    @pl.loop(0, most)
    def _(s):
        rows = pl.ds(pl.multiple_of(s * occupied, occupied), occupied)
        for label in range(IRREPS):
            for tile in range(tiles):
                acc[label, tile, rows, :] = jnp.zeros((occupied, LANES), jnp.float32)

    most = count[IRREPS]

    first_half = codes[IRREPS] == 0

    def paired(first, second):
        turned = pltpu.roll(second, LANES // 2, second.ndim - 1)
        mask = first_half if first.ndim == 2 else jnp.broadcast_to(first_half[None], first.shape)
        return jnp.where(mask, first, turned), jnp.where(mask, turned, first)

    def labels_of(step):
        c_label = vir_irrep[(place[0] + step // groups * cs) // TILE]
        return [jnp.bitwise_xor(c_label, vir_irrep[2 * (step % groups) + h]) for h in range(2)]

    def build(tp, step, base, slots):
        labels = labels_of(jnp.minimum(step, total - 1))
        z = jnp.where(first_half, codes[labels[0]], codes[labels[1]])
        masks = [z == x for x in range(IRREPS - 1)]
        held = step % 2
        for s in slots:
            ids = [table[(base + s) * IRREPS + x] for x in range(IRREPS)]
            merged = []
            for c in range(cs):
                out = t_buf[held, c, ids[IRREPS - 1]]
                for x in range(IRREPS - 1):
                    out = jnp.where(masks[x], t_buf[held, c, ids[x]], out)
                merged.append(out)
            for p in range(cs // 2):
                halves = paired(merged[2 * p], merged[2 * p + 1])
                for h in range(2):
                    tp[h, p, s * occupied:(s + 1) * occupied, :] = halves[h]

    def work(size, base, step, held, tp, following):
        rows_all = size * occupied
        labels = labels_of(step)
        at = pl.ds(pl.multiple_of(base * occupied, occupied), rows_all)
        bands = virtual // band
        for n in range(bands):
            blocks = [v_buf[held, c, n * band:(n + 1) * band] for c in range(cs)]
            pairs = [paired(blocks[2 * p], blocks[2 * p + 1]) for p in range(cs // 2)]
            for h in range(2):
                weights = jnp.concatenate([pair[h].reshape(2 * LANES, LANES) for pair in pairs], axis=1)
                rows = jnp.concatenate([tp[h, p, :rows_all, :] for p in range(cs // 2)], axis=1)
                part = lax.dot_general(
                    rows, weights, (((1,), (1,)), ((), ())), preferred_element_type=jnp.float32
                )
                acc[labels[h], 2 * n, at, :] += part[:, :LANES]
                acc[labels[h], 2 * n + 1, at, :] += part[:, LANES:]
            build(following, step + 1, base, range(n * size // bands, (n + 1) * size // bands))

    def run(size, base):
        wait_all(0, 0)
        build(tp_even, 0, base, range(size))

        @pl.loop(0, total // 2)
        def _(r):
            for held, tp, following in ((0, tp_even, tp_odd), (1, tp_odd, tp_even)):
                step = 2 * r + held

                @pl.when(step + 1 < total)
                def _():
                    start_all(1, step + 1)

                @pl.when(step + 2 < total)
                def _():
                    start_all(0, step + 2)

                wait_all(1, step)

                @pl.when(step + 1 < total)
                def _():
                    wait_all(0, step + 1)

                work(size, base, step, held, tp, following)

    def begin():
        start_all(0, 0)
        start_all(1, 0)
        start_all(0, 1)

    low = 0
    for size in SIZES:
        @pl.when((most > low) & (most <= size))
        def _(size=size):
            run(size, 0)
        low = size

    @pl.when(most > low)
    def _():
        @pl.loop(0, (most + CHUNK - 1) // CHUNK)
        def _(r):
            @pl.when(r > 0)
            def _():
                begin()

            run(CHUNK, r * CHUNK)

    @pl.loop(0, occupied)
    def _(i):
        x = occ_irrep[i]
        rows = pl.ds(pl.multiple_of(slot_of[i] * occupied, occupied), occupied)
        to = pl.ds(pl.multiple_of(i * occupied, occupied), occupied)
        hit = [ycode_ref[...] == jnp.bitwise_xor(x, label) for label in range(IRREPS - 1)]
        for tile in range(tiles):
            out = acc[IRREPS - 1, tile, rows, :]
            for label in range(IRREPS - 1):
                out = jnp.where(hit[label], acc[label, tile, rows, :], out)
            xs[tile, to, :] = out

    @pl.loop(0, occupied * occupied // LANES)
    def _(r):
        rows = pl.ds(pl.multiple_of(r * LANES, LANES), LANES)
        for tile in range(tiles):
            zs[tile * LANES:(tile + 1) * LANES, :] = xs[tile, rows, :].T
        for tile in range(tiles):
            mixed = jnp.concatenate(
                [zs[pl.ds(tile * per_tile + b, virtual, stride=virtual), :] for b in range(per_tile)], axis=0
            )
            acc[0, tile, rows, :] = mixed.T

    near = occ_local // 2
    for part in range(2):
        @pl.loop(0, occupied // occ_local * near)
        def _(r, part=part):
            i = r // near * occ_local + part * near + r % near
            there = jnp.bitwise_xor(r // near, place[1])
            if part == 0 and occupied == 4 * occ_local:
                there = there % 2 * 2 + there // 2
            to = pl.ds(pl.multiple_of(r % near * occupied, occupied), occupied)
            rows = pl.ds(pl.multiple_of(i * occupied, occupied), occupied)
            for far in range(tiles):
                tile = jnp.bitwise_xor(place[2], far)
                value = xs[tile, rows, :] + acc[0, tile, pl.ds(i, occupied, stride=occupied), :]
                out_refs[2 * part + far % 2][there, far // 2, to, :] = value


def ladder(amplitudes, ladder_integrals, occ_irrep, vir_tile_irrep, first_c, occ_at, vir_at, occ_local):
    occupied, _, cd_local = amplitudes.shape
    virtual = ladder_integrals.shape[0]
    local_c = cd_local // NV
    cs = math.gcd(local_c, TILE, 8)
    assert cs % 2 == 0 and local_c * NV == cd_local and occupied == virtual and LANES % virtual == 0
    steps = local_c // cs
    assert steps * (NV // LANES) % 2 == 0
    tiles = virtual * virtual // LANES
    place = jnp.stack([first_c, occ_at, vir_at]).astype(jnp.int32)
    ycode = jnp.broadcast_to(occ_irrep[:, None], (occupied, LANES)).astype(jnp.int32)

    piece = jax.ShapeDtypeStruct(
        (occupied // occ_local, tiles // 2, occ_local // 2 * occupied, LANES), jnp.float32
    )
    slots = -(-occupied // CHUNK) * CHUNK
    return pl.pallas_call(
        functools.partial(ladder_kernel, cs=cs, occ_local=occ_local, steps=steps),
        out_shape=(piece,) * 4,
        grid_spec=pltpu.PrefetchScalarGridSpec(
            num_scalar_prefetch=3,
            grid=(),
            in_specs=[pl.BlockSpec(memory_space=pltpu.VMEM)] + [pl.BlockSpec(memory_space=pl.ANY)] * 2,
            out_specs=(pl.BlockSpec(memory_space=pltpu.VMEM),) * 4,
            scratch_shapes=[
                pltpu.VMEM((2, cs, occupied, occupied, LANES), jnp.bfloat16),
                pltpu.VMEM((2, cs, virtual, virtual, LANES), jnp.bfloat16),
                pltpu.VMEM((IRREPS, tiles, slots * occupied, LANES), jnp.float32),
                pltpu.VMEM((2, cs // 2, CHUNK * occupied, LANES), jnp.bfloat16),
                pltpu.VMEM((2, cs // 2, CHUNK * occupied, LANES), jnp.bfloat16),
                pltpu.VMEM((tiles * LANES, LANES), jnp.float32),
                pltpu.VMEM((tiles, occupied * occupied, LANES), jnp.float32),
                pltpu.VMEM((IRREPS + 1, occupied, LANES), jnp.bfloat16),
                pltpu.SMEM((slots * IRREPS,), jnp.int32),
                pltpu.SMEM((occupied,), jnp.int32),
                pltpu.SMEM((8,), jnp.int32),
                pltpu.SemaphoreType.DMA((2, 2, cs)),
            ],
        ),
        compiler_params=pltpu.CompilerParams(vmem_limit_bytes=42 * 1024 * 1024),
    )(occ_irrep, vir_tile_irrep, place, ycode, amplitudes, ladder_integrals)


def swap(values, axis, bit):
    size = lax.axis_size(axis)
    return lax.ppermute(values, axis, [(n, n ^ bit) for n in range(size)])


def owned_sum(pieces):
    arrived = [swap(pieces[2 * part + 1], "vir", 1) for part in range(2)]
    order = [(1, 2), (2, 1)]
    near, first, second = [], [], []
    for part in range(2):
        kept, came = pieces[2 * part], arrived[part]
        low, far = lax.optimization_barrier((kept[:2] + came[:2], kept[2:] + came[2:]))
        near.append(low)
        first.append(swap(far, "occ", order[part][0]))
    for part in range(2):
        low, far = lax.optimization_barrier((near[part][0] + first[part][0], near[part][1] + first[part][1]))
        near[part] = low
        second.append(swap(far, "occ", order[part][1]))
    mine = jnp.stack([near[part] + second[part] for part in range(2)], axis=1)
    total = mine[0]
    for away in range(1, mine.shape[0]):
        total = total + swap(mine[away], "vir", 2 * away)
    return total


def local(amplitudes, ladder_integrals, driver, occ_energy, vir_energy, occ_irrep, vir_tile_irrep):
    occ_groups = lax.axis_size("occ")
    vir_groups = lax.axis_size("vir")
    occupied = amplitudes.shape[0]
    virtual = ladder_integrals.shape[0]
    occ_local = occupied // occ_groups
    vir_local = virtual // vir_groups
    rank = lax.axis_index(("occ", "vir"))
    occ_rank = lax.axis_index("occ")
    vir_rank = lax.axis_index("vir")
    first_c = rank * (amplitudes.shape[2] // NV)
    tiles = virtual * virtual // LANES
    direct = vir_groups == tiles == 8 and occ_groups == 4
    here = (occ_rank, vir_rank) if direct else (0 * occ_rank, 0 * vir_rank)
    pieces = ladder(amplitudes, ladder_integrals, occ_irrep, vir_tile_irrep, first_c, *here, occ_local)
    if direct:
        owned = owned_sum(pieces).reshape(occ_local, occupied, vir_local, virtual)
    else:
        halves = [jnp.stack([pieces[2 * p], pieces[2 * p + 1]], axis=2) for p in range(2)]
        if occ_groups == 4:
            halves[0] = halves[0][jnp.array([0, 2, 1, 3])]
        term = jnp.stack(halves, axis=3).transpose(1, 2, 0, 3, 4, 5).reshape(
            tiles, occ_groups, occ_local, occupied, vir_groups // tiles, vir_local, virtual
        )
        term = term.transpose(1, 0, 4, 2, 3, 5, 6).reshape(
            occ_groups * vir_groups, occ_local, occupied, vir_local, virtual
        )
        owned = lax.psum_scatter(term, ("occ", "vir"), scatter_dimension=0, tiled=True)[0]
    own_occ = lax.dynamic_slice_in_dim(occ_energy, occ_rank * occ_local, occ_local, 0)
    own_vir = lax.dynamic_slice_in_dim(vir_energy, vir_rank * vir_local, vir_local, 0)
    denom = (
        own_occ[:, None, None, None]
        + occ_energy[None, None, :, None]
        - own_vir[None, :, None, None]
        - vir_energy[None, None, None, :]
    )
    shaped = driver.reshape(occ_local, vir_local, occupied, virtual) + owned.transpose(0, 2, 1, 3)
    return (shaped / denom).reshape(occ_local, vir_local, occupied * virtual)


def solution(mesh):
    return jax.shard_map(
        local,
        mesh=mesh,
        in_specs=(
            P(None, None, ("occ", "vir")),
            P(None, None, ("occ", "vir")),
            P("occ", "vir", None),
            P(),
            P(),
            P(),
            P(),
        ),
        out_specs=P("occ", "vir", None),
        check_vma=False,
    )
```

profile of v0, /device:TPU:0, one launch (start us, length us, event | category | flops | bytes accessed | tf_op | source)
XLA Modules:
  0.0 94.8 jit_solution(2588465630571839354)
XLA Ops:
  0.0 0.1 pad_add_fusion.place
  0.1 0.7 broadcast_in_dim.2.ycode_ref
  0.8 0.0 copy-start
  0.8 0.7 copy-done
  1.5 0.0 copy-start.1
  1.5 0.7 copy-done.1
  2.1 0.0 copy-start.4
  2.1 0.0 copy-start.2
  2.1 0.0 copy-start.3
  2.1 51.0 %shard_map.73 = (f32[4,4,128,128]{3,2,1,0:T(8,128)S(1)}, f32[4,4,128,128]{3,2,1,0:T(8,128)S(1)}, f32[4,4,128,128]{3,2,1,0:T(8,128)S(1)}, f32[4,4,128,128]{3,2,1,0:T(8,128)S(1)}) custom-call(s32[32]{0:T(128)S(1)} %copy-done, s32[12]{0:T(128)S(1)} %copy-done.1, s32[3]{0:T(128)S(1)} %pad_add_fusion.place, s32[32,128]{1,0:T(8,128)S(1)} %broadcast_in_dim.2.ycode_ref, ...), custom_call_target="tpu_custom_call" | custom-call | tf_op jit(solution)/shard_map/pallas_call | solution.py:233
  53.2 0.5 collective-permute-start.3
  53.7 0.1 collective-permute-start
  53.8 2.2 %collective-permute-done.3 = f32[4,4,128,128]{3,2,1,0:T(8,128)S(1)} collective-permute-done((f32[4,4,128,128]{3,2,1,0:T(8,128)S(1)}, f32[4,4,128,128]{3,2,1,0:T(8,128)S(1)}, u32[]{:S(2)}, u32[]{:S(2)}) %collective-permute-start.3) | collective-permute-done | bytes 1048608 | tf_op jit(solution)/shard_map/ppermute | solution.py:262
  56.0 0.1 slice_add_fusion
  56.1 2.9 %collective-permute-start.4 = (f32[2,4,128,128]{3,2,1,0:T(8,128)S(1)}, f32[2,4,128,128]{3,2,1,0:T(8,128)S(1)}, u32[]{:S(2)}, u32[]{:S(2)}) collective-permute-start(f32[2,4,128,128]{3,2,1,0:T(8,128)S(1)} %get-tuple-element.26), channel_id=1, source_target_pairs={{0,16},{8,24},{16,0},{24,8},{1,17},{9,25},{17,1},{25,9},{2,18},{10... | collective-permute-start | bytes 1572872 | tf_op jit(solution)/shard_map/ppermute | solution.py:262
  59.0 0.0 collective-permute-done
  59.0 0.1 slice_add_fusion.2
  59.2 1.6 %collective-permute-start.1 = (f32[2,4,128,128]{3,2,1,0:T(8,128)S(1)}, f32[2,4,128,128]{3,2,1,0:T(8,128)S(1)}, u32[]{:S(2)}, u32[]{:S(2)}) collective-permute-start(f32[2,4,128,128]{3,2,1,0:T(8,128)S(1)} %get-tuple-element.20), channel_id=1, source_target_pairs={{0,8},{8,0},{16,24},{24,16},{1,9},{9,1},{17,25},{25,17},{2,10},{10... | collective-permute-start | bytes 1572872 | tf_op jit(solution)/shard_map/ppermute | solution.py:262
  60.7 0.0 copy-done.4
  60.7 0.1 dynamic_slice.6
  60.8 10.5 %collective-permute-done.4 = f32[2,4,128,128]{3,2,1,0:T(8,128)S(1)} collective-permute-done((f32[2,4,128,128]{3,2,1,0:T(8,128)S(1)}, f32[2,4,128,128]{3,2,1,0:T(8,128)S(1)}, u32[]{:S(2)}, u32[]{:S(2)}) %collective-permute-start.4) | collective-permute-done | bytes 524320 | tf_op jit(solution)/shard_map/ppermute | solution.py:262
  71.3 0.1 fusion.1
  71.3 1.8 %collective-permute-start.5 = (f32[4,128,128]{2,1,0:T(8,128)S(1)}, f32[4,128,128]{2,1,0:T(8,128)S(1)}, u32[]{:S(2)}, u32[]{:S(2)}) collective-permute-start(f32[4,128,128]{2,1,0:T(8,128)S(1)} %get-tuple-element.28), channel_id=1, source_target_pairs={{0,8},{8,0},{16,24},{24,16},{1,9},{9,1},{17,25},{25,17},{2,10},{10... | collective-permute-start | bytes 786440 | tf_op jit(solution)/shard_map/ppermute | solution.py:262
  73.1 0.0 collective-permute-done.1
  73.1 0.1 fusion.3
  73.2 1.6 %collective-permute-start.2 = (f32[4,128,128]{2,1,0:T(8,128)S(1)}, f32[4,128,128]{2,1,0:T(8,128)S(1)}, u32[]{:S(2)}, u32[]{:S(2)}) collective-permute-start(f32[4,128,128]{2,1,0:T(8,128)S(1)} %get-tuple-element.22), channel_id=1, source_target_pairs={{0,16},{8,24},{16,0},{24,8},{1,17},{9,25},{17,1},{25,9},{2,18},{10... | collective-permute-start | bytes 786440 | tf_op jit(solution)/shard_map/ppermute | solution.py:262
  74.8 0.1 broadcast_add_fusion
  74.8 0.0 copy-done.2
  74.8 0.2 reshape.53
  75.0 0.0 copy-done.3
  75.0 0.1 dynamic_slice.7
  75.1 4.1 %collective-permute-done.5 = f32[4,128,128]{2,1,0:T(8,128)S(1)} collective-permute-done((f32[4,128,128]{2,1,0:T(8,128)S(1)}, f32[4,128,128]{2,1,0:T(8,128)S(1)}, u32[]{:S(2)}, u32[]{:S(2)}) %collective-permute-start.5) | collective-permute-done | bytes 262176 | tf_op jit(solution)/shard_map/ppermute | solution.py:262
  79.3 1.2 %collective-permute-done.2 = f32[4,128,128]{2,1,0:T(8,128)S(1)} collective-permute-done((f32[4,128,128]{2,1,0:T(8,128)S(1)}, f32[4,128,128]{2,1,0:T(8,128)S(1)}, u32[]{:S(2)}, u32[]{:S(2)}) %collective-permute-start.2) | collective-permute-done | bytes 262176 | tf_op jit(solution)/shard_map/ppermute | solution.py:262
  80.5 1.7 %collective-permute-start.6 = (f32[2,128,128]{2,1,0:T(8,128)S(1)}, f32[2,128,128]{2,1,0:T(8,128)S(1)}, u32[]{:S(2)}, u32[]{:S(2)}) collective-permute-start(f32[2,128,128]{2,1,0:T(8,128)S(1)} %get-tuple-element.37), channel_id=1, source_target_pairs={{0,2},{1,3},{2,0},{3,1},{4,6},{5,7},{6,4},{7,5},{8,10},{9,11},{10,... | collective-permute-start | bytes 393224 | tf_op jit(solution)/shard_map/ppermute | solution.py:262
  82.2 2.6 %collective-permute-start.7 = (f32[2,128,128]{2,1,0:T(8,128)S(1)}, f32[2,128,128]{2,1,0:T(8,128)S(1)}, u32[]{:S(2)}, u32[]{:S(2)}) collective-permute-start(f32[2,128,128]{2,1,0:T(8,128)S(1)} %get-tuple-element.39), channel_id=1, source_target_pairs={{0,4},{1,5},{2,6},{3,7},{4,0},{5,1},{6,2},{7,3},{8,12},{9,13},{10,... | collective-permute-start | bytes 393224 | tf_op jit(solution)/shard_map/ppermute | solution.py:262
  84.8 0.2 collective-permute-start.8
  85.0 0.1 broadcast_subtract_fusion
  85.1 1.2 %collective-permute-done.6 = f32[2,128,128]{2,1,0:T(8,128)S(1)} collective-permute-done((f32[2,128,128]{2,1,0:T(8,128)S(1)}, f32[2,128,128]{2,1,0:T(8,128)S(1)}, u32[]{:S(2)}, u32[]{:S(2)}) %collective-permute-start.6) | collective-permute-done | bytes 131104 | tf_op jit(solution)/shard_map/ppermute | solution.py:262
  86.2 7.1 %collective-permute-done.7 = f32[2,128,128]{2,1,0:T(8,128)S(1)} collective-permute-done((f32[2,128,128]{2,1,0:T(8,128)S(1)}, f32[2,128,128]{2,1,0:T(8,128)S(1)}, u32[]{:S(2)}, u32[]{:S(2)}) %collective-permute-start.7) | collective-permute-done | bytes 131104 | tf_op jit(solution)/shard_map/ppermute | solution.py:262
  93.3 0.0 collective-permute-done.8
  93.4 0.3 reshape.54
  93.6 0.2 fusion
  93.9 0.9 reshape.55
  (4 shorter events, 0.1 us)
Async XLA Ops:
  0.8 0.7 copy-start
  1.5 0.7 copy-start.1
  2.1 58.6 %copy-start.4 = (f32[32]{0:T(128)S(1)}, f32[32]{0:T(128)}, u32[]{:S(2)}) copy-start(f32[32]{0:T(128)} %param.10) | copy-start | bytes 388
  2.1 72.7 %copy-start.2 = (f32[8,4,1024]{2,1,0:T(4,128)S(1)}, f32[8,4,1024]{2,1,0:T(4,128)}, u32[]{:S(2)}) copy-start(f32[8,4,1024]{2,1,0:T(4,128)} %param.9) | copy-start | bytes 393220
  2.1 72.9 %copy-start.3 = (f32[32]{0:T(128)S(1)}, f32[32]{0:T(128)}, u32[]{:S(2)}) copy-start(f32[32]{0:T(128)} %param.11) | copy-start | bytes 388
  53.2 2.8 %collective-permute-start.3 = (f32[4,4,128,128]{3,2,1,0:T(8,128)S(1)}, f32[4,4,128,128]{3,2,1,0:T(8,128)S(1)}, u32[]{:S(2)}, u32[]{:S(2)}) collective-permute-start(f32[4,4,128,128]{3,2,1,0:T(8,128)S(1)} %get-tuple-element.24), channel_id=1, source_target_pairs={{0,1},{1,0},{2,3},{3,2},{4,5},{5,4},{6,7},{7,6},{8,9},{9,8},{10,11... | collective-permute-start | bytes 3145736 | tf_op jit(solution)/shard_map/ppermute | solution.py:262
  53.7 5.3 %collective-permute-start = (f32[4,4,128,128]{3,2,1,0:T(8,128)S(1)}, f32[4,4,128,128]{3,2,1,0:T(8,128)S(1)}, u32[]{:S(2)}, u32[]{:S(2)}) collective-permute-start(f32[4,4,128,128]{3,2,1,0:T(8,128)S(1)} %get-tuple-element.18), channel_id=1, source_target_pairs={{0,1},{1,0},{2,3},{3,2},{4,5},{5,4},{6,7},{7,6},{8,9},{9,8},{10,11... | collective-permute-start | bytes 3145736 | tf_op jit(solution)/shard_map/ppermute | solution.py:262
  56.1 15.2 %collective-permute-start.4 = (f32[2,4,128,128]{3,2,1,0:T(8,128)S(1)}, f32[2,4,128,128]{3,2,1,0:T(8,128)S(1)}, u32[]{:S(2)}, u32[]{:S(2)}) collective-permute-start(f32[2,4,128,128]{3,2,1,0:T(8,128)S(1)} %get-tuple-element.26), channel_id=1, source_target_pairs={{0,16},{8,24},{16,0},{24,8},{1,17},{9,25},{17,1},{25,9},{2,18},{10... | collective-permute-start | bytes 1572872 | tf_op jit(solution)/shard_map/ppermute | solution.py:262
  59.2 13.9 %collective-permute-start.1 = (f32[2,4,128,128]{3,2,1,0:T(8,128)S(1)}, f32[2,4,128,128]{3,2,1,0:T(8,128)S(1)}, u32[]{:S(2)}, u32[]{:S(2)}) collective-permute-start(f32[2,4,128,128]{3,2,1,0:T(8,128)S(1)} %get-tuple-element.20), channel_id=1, source_target_pairs={{0,8},{8,0},{16,24},{24,16},{1,9},{9,1},{17,25},{25,17},{2,10},{10... | collective-permute-start | bytes 1572872 | tf_op jit(solution)/shard_map/ppermute | solution.py:262
  71.3 7.9 %collective-permute-start.5 = (f32[4,128,128]{2,1,0:T(8,128)S(1)}, f32[4,128,128]{2,1,0:T(8,128)S(1)}, u32[]{:S(2)}, u32[]{:S(2)}) collective-permute-start(f32[4,128,128]{2,1,0:T(8,128)S(1)} %get-tuple-element.28), channel_id=1, source_target_pairs={{0,8},{8,0},{16,24},{24,16},{1,9},{9,1},{17,25},{25,17},{2,10},{10... | collective-permute-start | bytes 786440 | tf_op jit(solution)/shard_map/ppermute | solution.py:262
  73.2 7.3 %collective-permute-start.2 = (f32[4,128,128]{2,1,0:T(8,128)S(1)}, f32[4,128,128]{2,1,0:T(8,128)S(1)}, u32[]{:S(2)}, u32[]{:S(2)}) collective-permute-start(f32[4,128,128]{2,1,0:T(8,128)S(1)} %get-tuple-element.22), channel_id=1, source_target_pairs={{0,16},{8,24},{16,0},{24,8},{1,17},{9,25},{17,1},{25,9},{2,18},{10... | collective-permute-start | bytes 786440 | tf_op jit(solution)/shard_map/ppermute | solution.py:262
  80.5 5.7 %collective-permute-start.6 = (f32[2,128,128]{2,1,0:T(8,128)S(1)}, f32[2,128,128]{2,1,0:T(8,128)S(1)}, u32[]{:S(2)}, u32[]{:S(2)}) collective-permute-start(f32[2,128,128]{2,1,0:T(8,128)S(1)} %get-tuple-element.37), channel_id=1, source_target_pairs={{0,2},{1,3},{2,0},{3,1},{4,6},{5,7},{6,4},{7,5},{8,10},{9,11},{10,... | collective-permute-start | bytes 393224 | tf_op jit(solution)/shard_map/ppermute | solution.py:262
  82.2 11.2 %collective-permute-start.7 = (f32[2,128,128]{2,1,0:T(8,128)S(1)}, f32[2,128,128]{2,1,0:T(8,128)S(1)}, u32[]{:S(2)}, u32[]{:S(2)}) collective-permute-start(f32[2,128,128]{2,1,0:T(8,128)S(1)} %get-tuple-element.39), channel_id=1, source_target_pairs={{0,4},{1,5},{2,6},{3,7},{4,0},{5,1},{6,2},{7,3},{8,12},{9,13},{10,... | collective-permute-start | bytes 393224 | tf_op jit(solution)/shard_map/ppermute | solution.py:262
  84.8 8.6 %collective-permute-start.8 = (f32[2,128,128]{2,1,0:T(8,128)S(1)}, f32[2,128,128]{2,1,0:T(8,128)S(1)}, u32[]{:S(2)}, u32[]{:S(2)}) collective-permute-start(f32[2,128,128]{2,1,0:T(8,128)S(1)} %get-tuple-element.38), channel_id=1, source_target_pairs={{0,6},{1,7},{2,4},{3,5},{4,2},{5,3},{6,0},{7,1},{8,14},{9,15},{10,... | collective-permute-start | bytes 393224 | tf_op jit(solution)/shard_map/ppermute | solution.py:262
where the time goes:
time: 93.2 us; the launch traced here: 94.8 us
  Pallas kernels  51 us (55%)
  waiting for transfers between devices  26.3 us (28%)
  starting transfers between devices  12.9 us (14%)
  local copies, waits for them, and re-layouts  3.56 us (4%)
    pallas_call x1, Pallas kernels, ladder(): pl.pallas_call(functools.partial(ladder_kernel, cs=cs, occ_local=occ_loca...  51 us
    ppermute x9, waiting for transfers between devices, swap(): return lax.ppermute(values, axis, [(n, n ^ bit) for n in range(size)])  26.3 us
    ppermute x9, starting transfers between devices, swap(): return lax.ppermute(values, axis, [(n, n ^ bit) for n in range(size)])  12.9 us
  transfers between devices with their start and end apart: 9, of which 6 were waited for; matrix products, arithmetic and copies ran while one was open for 1% of the time, Pallas kernels for 0%

commit v1 on v0

--- a/solution.py
+++ b/solution.py
@@ -16,10 +16,11 @@
 CHUNK = 16
 
 
-def ladder_kernel(occ_irrep, vir_irrep, place, ycode_ref, t_hbm, v_hbm, *refs, cs, occ_local, steps):
+def ladder_kernel(facts, ycode_ref, t_hbm, v_hbm, *refs, cs, occ_local, steps):
     out_refs = refs[:4]
     t_buf, v_buf, acc, tp_even, tp_odd, zs, xs, codes, table, slot_of, count, sems = refs[4:]
     occupied = t_hbm.shape[0]
+    place, occ_irrep, vir_irrep = (facts.at[pl.ds(n, many)] for n, many in ((0, 8), (8, occupied), (8 + occupied, NV // TILE)))
     virtual = v_hbm.shape[0]
     groups = NV // LANES
     tiles = virtual * virtual // LANES
@@ -82,10 +83,11 @@
     most = count[IRREPS]
 
     first_half = codes[IRREPS] == 0
+    first_turned = pltpu.roll(codes[IRREPS], LANES // 2, 1) == 1
 
     def paired(first, second):
         turned = pltpu.roll(second, LANES // 2, second.ndim - 1)
-        mask = first_half if first.ndim == 2 else jnp.broadcast_to(first_half[None], first.shape)
+        mask = first_half if first.ndim == 2 else jnp.broadcast_to(first_turned[None], first.shape)
         return jnp.where(mask, first, turned), jnp.where(mask, turned, first)
 
     def labels_of(step):
@@ -223,7 +225,8 @@
     steps = local_c // cs
     assert steps * (NV // LANES) % 2 == 0
     tiles = virtual * virtual // LANES
-    place = jnp.stack([first_c, occ_at, vir_at]).astype(jnp.int32)
+    place = jnp.stack([first_c, occ_at, vir_at] + [0 * occ_at] * 5)
+    facts = jnp.concatenate([place, occ_irrep, vir_tile_irrep]).astype(jnp.int32)
     ycode = jnp.broadcast_to(occ_irrep[:, None], (occupied, LANES)).astype(jnp.int32)
 
     piece = jax.ShapeDtypeStruct(
@@ -234,7 +237,7 @@
         functools.partial(ladder_kernel, cs=cs, occ_local=occ_local, steps=steps),
         out_shape=(piece,) * 4,
         grid_spec=pltpu.PrefetchScalarGridSpec(
-            num_scalar_prefetch=3,
+            num_scalar_prefetch=1,
             grid=(),
             in_specs=[pl.BlockSpec(memory_space=pltpu.VMEM)] + [pl.BlockSpec(memory_space=pl.ANY)] * 2,
             out_specs=(pl.BlockSpec(memory_space=pltpu.VMEM),) * 4,
@@ -254,7 +257,7 @@
             ],
         ),
         compiler_params=pltpu.CompilerParams(vmem_limit_bytes=42 * 1024 * 1024),
-    )(occ_irrep, vir_tile_irrep, place, ycode, amplitudes, ladder_integrals)
+    )(facts, ycode, amplitudes, ladder_integrals)
 
 
 def swap(values, axis, bit):

time: 93.2 us -> 90.5 us (0.971); the launches traced: 94.8 us -> 90.3 us
  Pallas kernels: 51 us -> 47.2 us
    pallas_call x1, Pallas kernels: 51 us -> 47.2 us  [ladder(): pl.pallas_call(functools.partial(ladder_kernel, cs=cs, occ_local=occ_loca...]
    unnamed x10 -> x6, local copies, waits for them, and re-layouts: 1.32 us -> 0.01 us
where the time goes in v1:
time: 90.5 us; the launch traced here: 90.3 us
  Pallas kernels  47.2 us (52%)
  waiting for transfers between devices  26.3 us (29%)
  starting transfers between devices  12.9 us (14%)
  local copies, waits for them, and re-layouts  3 us (3%)
    pallas_call x1, Pallas kernels, ladder(): pl.pallas_call(functools.partial(ladder_kernel, cs=cs, occ_local=occ_loca...  47.2 us
    ppermute x9, waiting for transfers between devices, swap(): return lax.ppermute(values, axis, [(n, n ^ bit) for n in range(size)])  26.3 us
    ppermute x9, starting transfers between devices, swap(): return lax.ppermute(values, axis, [(n, n ^ bit) for n in range(size)])  12.9 us
  transfers between devices with their start and end apart: 9, of which 6 were waited for; matrix products, arithmetic and copies ran while one was open for 1% of the time, Pallas kernels for 0%

profile of v1, /device:TPU:0, one launch (start us, length us, event | category | flops | bytes accessed | tf_op | source)
XLA Modules:
  0.0 90.3 jit_solution(16354803012792283124)
XLA Ops:
  0.0 0.7 concatenate.3.facts
  0.7 0.7 broadcast_in_dim.2.ycode_ref
  1.5 0.0 copy-start.2
  1.5 0.0 copy-start
  1.5 0.0 copy-start.1
  1.5 47.2 %shard_map.73 = (f32[4,4,128,128]{3,2,1,0:T(8,128)S(1)}, f32[4,4,128,128]{3,2,1,0:T(8,128)S(1)}, f32[4,4,128,128]{3,2,1,0:T(8,128)S(1)}, f32[4,4,128,128]{3,2,1,0:T(8,128)S(1)}) custom-call(s32[52]{0:T(128)S(1)} %concatenate.3.facts, s32[32,128]{1,0:T(8,128)S(1)} %broadcast_in_dim.2.ycode_ref, bf16[32,32,18432]{2,1,0:T(8,128)(2,1)} %t_hbm.1, ...), custom_call_target="tpu_custom_call" | custom-call | tf_op jit(solution)/shard_map/pallas_call | solution.py:236
  48.7 0.5 collective-permute-start.3
  49.2 0.1 collective-permute-start
  49.2 2.2 %collective-permute-done.3 = f32[4,4,128,128]{3,2,1,0:T(8,128)S(1)} collective-permute-done((f32[4,4,128,128]{3,2,1,0:T(8,128)S(1)}, f32[4,4,128,128]{3,2,1,0:T(8,128)S(1)}, u32[]{:S(2)}, u32[]{:S(2)}) %collective-permute-start.3) | collective-permute-done | bytes 1048608 | tf_op jit(solution)/shard_map/ppermute | solution.py:265
  51.5 0.1 slice_add_fusion
  51.6 3.0 %collective-permute-start.4 = (f32[2,4,128,128]{3,2,1,0:T(8,128)S(1)}, f32[2,4,128,128]{3,2,1,0:T(8,128)S(1)}, u32[]{:S(2)}, u32[]{:S(2)}) collective-permute-start(f32[2,4,128,128]{3,2,1,0:T(8,128)S(1)} %get-tuple-element.26), channel_id=1, source_target_pairs={{0,16},{8,24},{16,0},{24,8},{1,17},{9,25},{17,1},{25,9},{2,18},{10... | collective-permute-start | bytes 1572872 | tf_op jit(solution)/shard_map/ppermute | solution.py:265
  54.5 0.0 collective-permute-done
  54.5 0.1 slice_add_fusion.2
  54.7 1.6 %collective-permute-start.1 = (f32[2,4,128,128]{3,2,1,0:T(8,128)S(1)}, f32[2,4,128,128]{3,2,1,0:T(8,128)S(1)}, u32[]{:S(2)}, u32[]{:S(2)}) collective-permute-start(f32[2,4,128,128]{3,2,1,0:T(8,128)S(1)} %get-tuple-element.20), channel_id=1, source_target_pairs={{0,8},{8,0},{16,24},{24,16},{1,9},{9,1},{17,25},{25,17},{2,10},{10... | collective-permute-start | bytes 1572872 | tf_op jit(solution)/shard_map/ppermute | solution.py:265
  56.2 0.0 copy-done.2
  56.2 0.1 dynamic_slice.6
  56.3 10.5 %collective-permute-done.4 = f32[2,4,128,128]{3,2,1,0:T(8,128)S(1)} collective-permute-done((f32[2,4,128,128]{3,2,1,0:T(8,128)S(1)}, f32[2,4,128,128]{3,2,1,0:T(8,128)S(1)}, u32[]{:S(2)}, u32[]{:S(2)}) %collective-permute-start.4) | collective-permute-done | bytes 524320 | tf_op jit(solution)/shard_map/ppermute | solution.py:265
  66.8 0.1 fusion.1
  66.8 1.8 %collective-permute-start.5 = (f32[4,128,128]{2,1,0:T(8,128)S(1)}, f32[4,128,128]{2,1,0:T(8,128)S(1)}, u32[]{:S(2)}, u32[]{:S(2)}) collective-permute-start(f32[4,128,128]{2,1,0:T(8,128)S(1)} %get-tuple-element.28), channel_id=1, source_target_pairs={{0,8},{8,0},{16,24},{24,16},{1,9},{9,1},{17,25},{25,17},{2,10},{10... | collective-permute-start | bytes 786440 | tf_op jit(solution)/shard_map/ppermute | solution.py:265
  68.6 0.0 collective-permute-done.1
  68.6 0.1 fusion.3
  68.7 1.6 %collective-permute-start.2 = (f32[4,128,128]{2,1,0:T(8,128)S(1)}, f32[4,128,128]{2,1,0:T(8,128)S(1)}, u32[]{:S(2)}, u32[]{:S(2)}) collective-permute-start(f32[4,128,128]{2,1,0:T(8,128)S(1)} %get-tuple-element.22), channel_id=1, source_target_pairs={{0,16},{8,24},{16,0},{24,8},{1,17},{9,25},{17,1},{25,9},{2,18},{10... | collective-permute-start | bytes 786440 | tf_op jit(solution)/shard_map/ppermute | solution.py:265
  70.2 0.1 broadcast_add_fusion
  70.3 0.0 copy-done
  70.3 0.2 reshape.53
  70.5 0.0 copy-done.1
  70.5 0.1 dynamic_slice.7
  70.6 4.1 %collective-permute-done.5 = f32[4,128,128]{2,1,0:T(8,128)S(1)} collective-permute-done((f32[4,128,128]{2,1,0:T(8,128)S(1)}, f32[4,128,128]{2,1,0:T(8,128)S(1)}, u32[]{:S(2)}, u32[]{:S(2)}) %collective-permute-start.5) | collective-permute-done | bytes 262176 | tf_op jit(solution)/shard_map/ppermute | solution.py:265
  74.8 1.2 %collective-permute-done.2 = f32[4,128,128]{2,1,0:T(8,128)S(1)} collective-permute-done((f32[4,128,128]{2,1,0:T(8,128)S(1)}, f32[4,128,128]{2,1,0:T(8,128)S(1)}, u32[]{:S(2)}, u32[]{:S(2)}) %collective-permute-start.2) | collective-permute-done | bytes 262176 | tf_op jit(solution)/shard_map/ppermute | solution.py:265
  76.0 1.6 %collective-permute-start.6 = (f32[2,128,128]{2,1,0:T(8,128)S(1)}, f32[2,128,128]{2,1,0:T(8,128)S(1)}, u32[]{:S(2)}, u32[]{:S(2)}) collective-permute-start(f32[2,128,128]{2,1,0:T(8,128)S(1)} %get-tuple-element.37), channel_id=1, source_target_pairs={{0,2},{1,3},{2,0},{3,1},{4,6},{5,7},{6,4},{7,5},{8,10},{9,11},{10,... | collective-permute-start | bytes 393224 | tf_op jit(solution)/shard_map/ppermute | solution.py:265
  77.7 2.6 %collective-permute-start.7 = (f32[2,128,128]{2,1,0:T(8,128)S(1)}, f32[2,128,128]{2,1,0:T(8,128)S(1)}, u32[]{:S(2)}, u32[]{:S(2)}) collective-permute-start(f32[2,128,128]{2,1,0:T(8,128)S(1)} %get-tuple-element.39), channel_id=1, source_target_pairs={{0,4},{1,5},{2,6},{3,7},{4,0},{5,1},{6,2},{7,3},{8,12},{9,13},{10,... | collective-permute-start | bytes 393224 | tf_op jit(solution)/shard_map/ppermute | solution.py:265
  80.3 0.2 collective-permute-start.8
  80.5 0.1 broadcast_subtract_fusion
  80.6 1.2 %collective-permute-done.6 = f32[2,128,128]{2,1,0:T(8,128)S(1)} collective-permute-done((f32[2,128,128]{2,1,0:T(8,128)S(1)}, f32[2,128,128]{2,1,0:T(8,128)S(1)}, u32[]{:S(2)}, u32[]{:S(2)}) %collective-permute-start.6) | collective-permute-done | bytes 131104 | tf_op jit(solution)/shard_map/ppermute | solution.py:265
  81.8 7.1 %collective-permute-done.7 = f32[2,128,128]{2,1,0:T(8,128)S(1)} collective-permute-done((f32[2,128,128]{2,1,0:T(8,128)S(1)}, f32[2,128,128]{2,1,0:T(8,128)S(1)}, u32[]{:S(2)}, u32[]{:S(2)}) %collective-permute-start.7) | collective-permute-done | bytes 131104 | tf_op jit(solution)/shard_map/ppermute | solution.py:265
  88.8 0.0 collective-permute-done.8
  88.9 0.3 reshape.54
  89.1 0.2 fusion
  89.3 0.9 %reshape.55 = f32[8,4,1024]{2,1,0:T(4,128)} reshape(f32[8,4,32,32]{3,2,1,0:T(8,128)S(1)} %fusion) | data formatting | bytes 262144 | tf_op jit(solution)/shard_map/reshape | solution.py:325
  (5 shorter events, 0.1 us)
Async XLA Ops:
  1.5 54.7 %copy-start.2 = (f32[32]{0:T(128)S(1)}, f32[32]{0:T(128)}, u32[]{:S(2)}) copy-start(f32[32]{0:T(128)} %param.10) | copy-start | bytes 388
  1.5 68.8 %copy-start = (f32[8,4,1024]{2,1,0:T(4,128)S(1)}, f32[8,4,1024]{2,1,0:T(4,128)}, u32[]{:S(2)}) copy-start(f32[8,4,1024]{2,1,0:T(4,128)} %param.9) | copy-start | bytes 393220
  1.5 69.0 %copy-start.1 = (f32[32]{0:T(128)S(1)}, f32[32]{0:T(128)}, u32[]{:S(2)}) copy-start(f32[32]{0:T(128)} %param.11) | copy-start | bytes 388
  48.7 2.8 %collective-permute-start.3 = (f32[4,4,128,128]{3,2,1,0:T(8,128)S(1)}, f32[4,4,128,128]{3,2,1,0:T(8,128)S(1)}, u32[]{:S(2)}, u32[]{:S(2)}) collective-permute-start(f32[4,4,128,128]{3,2,1,0:T(8,128)S(1)} %get-tuple-element.24), channel_id=1, source_target_pairs={{0,1},{1,0},{2,3},{3,2},{4,5},{5,4},{6,7},{7,6},{8,9},{9,8},{10,11... | collective-permute-start | bytes 3145736 | tf_op jit(solution)/shard_map/ppermute | solution.py:265
  49.2 5.4 %collective-permute-start = (f32[4,4,128,128]{3,2,1,0:T(8,128)S(1)}, f32[4,4,128,128]{3,2,1,0:T(8,128)S(1)}, u32[]{:S(2)}, u32[]{:S(2)}) collective-permute-start(f32[4,4,128,128]{3,2,1,0:T(8,128)S(1)} %get-tuple-element.18), channel_id=1, source_target_pairs={{0,1},{1,0},{2,3},{3,2},{4,5},{5,4},{6,7},{7,6},{8,9},{9,8},{10,11... | collective-permute-start | bytes 3145736 | tf_op jit(solution)/shard_map/ppermute | solution.py:265
  51.6 15.2 %collective-permute-start.4 = (f32[2,4,128,128]{3,2,1,0:T(8,128)S(1)}, f32[2,4,128,128]{3,2,1,0:T(8,128)S(1)}, u32[]{:S(2)}, u32[]{:S(2)}) collective-permute-start(f32[2,4,128,128]{3,2,1,0:T(8,128)S(1)} %get-tuple-element.26), channel_id=1, source_target_pairs={{0,16},{8,24},{16,0},{24,8},{1,17},{9,25},{17,1},{25,9},{2,18},{10... | collective-permute-start | bytes 1572872 | tf_op jit(solution)/shard_map/ppermute | solution.py:265
  54.7 13.9 %collective-permute-start.1 = (f32[2,4,128,128]{3,2,1,0:T(8,128)S(1)}, f32[2,4,128,128]{3,2,1,0:T(8,128)S(1)}, u32[]{:S(2)}, u32[]{:S(2)}) collective-permute-start(f32[2,4,128,128]{3,2,1,0:T(8,128)S(1)} %get-tuple-element.20), channel_id=1, source_target_pairs={{0,8},{8,0},{16,24},{24,16},{1,9},{9,1},{17,25},{25,17},{2,10},{10... | collective-permute-start | bytes 1572872 | tf_op jit(solution)/shard_map/ppermute | solution.py:265
  66.8 7.9 %collective-permute-start.5 = (f32[4,128,128]{2,1,0:T(8,128)S(1)}, f32[4,128,128]{2,1,0:T(8,128)S(1)}, u32[]{:S(2)}, u32[]{:S(2)}) collective-permute-start(f32[4,128,128]{2,1,0:T(8,128)S(1)} %get-tuple-element.28), channel_id=1, source_target_pairs={{0,8},{8,0},{16,24},{24,16},{1,9},{9,1},{17,25},{25,17},{2,10},{10... | collective-permute-start | bytes 786440 | tf_op jit(solution)/shard_map/ppermute | solution.py:265
  68.7 7.3 %collective-permute-start.2 = (f32[4,128,128]{2,1,0:T(8,128)S(1)}, f32[4,128,128]{2,1,0:T(8,128)S(1)}, u32[]{:S(2)}, u32[]{:S(2)}) collective-permute-start(f32[4,128,128]{2,1,0:T(8,128)S(1)} %get-tuple-element.22), channel_id=1, source_target_pairs={{0,16},{8,24},{16,0},{24,8},{1,17},{9,25},{17,1},{25,9},{2,18},{10... | collective-permute-start | bytes 786440 | tf_op jit(solution)/shard_map/ppermute | solution.py:265
  76.0 5.7 %collective-permute-start.6 = (f32[2,128,128]{2,1,0:T(8,128)S(1)}, f32[2,128,128]{2,1,0:T(8,128)S(1)}, u32[]{:S(2)}, u32[]{:S(2)}) collective-permute-start(f32[2,128,128]{2,1,0:T(8,128)S(1)} %get-tuple-element.37), channel_id=1, source_target_pairs={{0,2},{1,3},{2,0},{3,1},{4,6},{5,7},{6,4},{7,5},{8,10},{9,11},{10,... | collective-permute-start | bytes 393224 | tf_op jit(solution)/shard_map/ppermute | solution.py:265
  77.7 11.2 %collective-permute-start.7 = (f32[2,128,128]{2,1,0:T(8,128)S(1)}, f32[2,128,128]{2,1,0:T(8,128)S(1)}, u32[]{:S(2)}, u32[]{:S(2)}) collective-permute-start(f32[2,128,128]{2,1,0:T(8,128)S(1)} %get-tuple-element.39), channel_id=1, source_target_pairs={{0,4},{1,5},{2,6},{3,7},{4,0},{5,1},{6,2},{7,3},{8,12},{9,13},{10,... | collective-permute-start | bytes 393224 | tf_op jit(solution)/shard_map/ppermute | solution.py:265
  80.3 8.6 %collective-permute-start.8 = (f32[2,128,128]{2,1,0:T(8,128)S(1)}, f32[2,128,128]{2,1,0:T(8,128)S(1)}, u32[]{:S(2)}, u32[]{:S(2)}) collective-permute-start(f32[2,128,128]{2,1,0:T(8,128)S(1)} %get-tuple-element.38), channel_id=1, source_target_pairs={{0,6},{1,7},{2,4},{3,5},{4,2},{5,3},{6,0},{7,1},{8,14},{9,15},{10,... | collective-permute-start | bytes 393224 | tf_op jit(solution)/shard_map/ppermute | solution.py:265

commit v2 on v1

--- a/solution.py
+++ b/solution.py
@@ -28,15 +28,18 @@
     lane = lax.broadcasted_iota(jnp.int32, (occupied, LANES), 1)
     band = 2 * LANES // virtual
 
-    total = steps * groups
-
-    def copies(which, step):
+    per_block = 2
+    wide = per_block * LANES
+    blocks_c = groups // per_block
+    total = steps * blocks_c
+
+    def copies(which, block):
         src, dst = ((t_hbm, t_buf), (v_hbm, v_buf))[which]
         made = []
         for c in range(cs):
-            start = pl.multiple_of((step // groups * cs + c) * NV + step % groups * LANES, LANES)
+            start = pl.multiple_of((block // blocks_c * cs + c) * NV + block % blocks_c * wide, LANES)
             made.append(pltpu.make_async_copy(
-                src.at[:, :, pl.ds(start, LANES)], dst.at[step % 2, c], sems.at[step % 2, which, c]
+                src.at[:, :, pl.ds(start, wide)], dst.at[block % 2, c], sems.at[block % 2, which, c]
             ))
         return made
 
@@ -90,35 +93,39 @@
         mask = first_half if first.ndim == 2 else jnp.broadcast_to(first_turned[None], first.shape)
         return jnp.where(mask, first, turned), jnp.where(mask, turned, first)
 
-    def labels_of(step):
-        c_label = vir_irrep[(place[0] + step // groups * cs) // TILE]
-        return [jnp.bitwise_xor(c_label, vir_irrep[2 * (step % groups) + h]) for h in range(2)]
-
-    def build(tp, step, base, slots):
-        labels = labels_of(jnp.minimum(step, total - 1))
+    def labels_of(block, m):
+        c_label = vir_irrep[(place[0] + block // blocks_c * cs) // TILE]
+        first = 2 * (block % blocks_c * per_block + m)
+        return [jnp.bitwise_xor(c_label, vir_irrep[first + h]) for h in range(2)]
+
+    def build(tp, block, m, base, slots):
+        labels = labels_of(jnp.minimum(block, total - 1), m)
+        lanes = slice(m * LANES, (m + 1) * LANES)
         z = jnp.where(first_half, codes[labels[0]], codes[labels[1]])
         masks = [z == x for x in range(IRREPS - 1)]
-        held = step % 2
+        held = block % 2
         for s in slots:
             ids = [table[(base + s) * IRREPS + x] for x in range(IRREPS)]
             merged = []
             for c in range(cs):
-                out = t_buf[held, c, ids[IRREPS - 1]]
+                out = t_buf[held, c, ids[IRREPS - 1], :, lanes]
                 for x in range(IRREPS - 1):
-                    out = jnp.where(masks[x], t_buf[held, c, ids[x]], out)
+                    out = jnp.where(masks[x], t_buf[held, c, ids[x], :, lanes], out)
                 merged.append(out)
             for p in range(cs // 2):
                 halves = paired(merged[2 * p], merged[2 * p + 1])
                 for h in range(2):
                     tp[h, p, s * occupied:(s + 1) * occupied, :] = halves[h]
 
-    def work(size, base, step, held, tp, following):
+    def work(size, base, block, m, tp, following):
         rows_all = size * occupied
-        labels = labels_of(step)
+        labels = labels_of(block, m)
+        held = block % 2
+        lanes = slice(m * LANES, (m + 1) * LANES)
         at = pl.ds(pl.multiple_of(base * occupied, occupied), rows_all)
         bands = virtual // band
         for n in range(bands):
-            blocks = [v_buf[held, c, n * band:(n + 1) * band] for c in range(cs)]
+            blocks = [v_buf[held, c, n * band:(n + 1) * band, :, lanes] for c in range(cs)]
             pairs = [paired(blocks[2 * p], blocks[2 * p + 1]) for p in range(cs // 2)]
             for h in range(2):
                 weights = jnp.concatenate([pair[h].reshape(2 * LANES, LANES) for pair in pairs], axis=1)
@@ -128,32 +135,30 @@
                 )
                 acc[labels[h], 2 * n, at, :] += part[:, :LANES]
                 acc[labels[h], 2 * n + 1, at, :] += part[:, LANES:]
-            build(following, step + 1, base, range(n * size // bands, (n + 1) * size // bands))
+            build(following, block + m, 1 - m, base, range(n * size // bands, (n + 1) * size // bands))
 
     def run(size, base):
         wait_all(0, 0)
-        build(tp_even, 0, base, range(size))
-
-        @pl.loop(0, total // 2)
-        def _(r):
-            for held, tp, following in ((0, tp_even, tp_odd), (1, tp_odd, tp_even)):
-                step = 2 * r + held
-
-                @pl.when(step + 1 < total)
-                def _():
-                    start_all(1, step + 1)
-
-                @pl.when(step + 2 < total)
-                def _():
-                    start_all(0, step + 2)
-
-                wait_all(1, step)
-
-                @pl.when(step + 1 < total)
-                def _():
-                    wait_all(0, step + 1)
-
-                work(size, base, step, held, tp, following)
+        build(tp_even, 0, 0, base, range(size))
+
+        @pl.loop(0, total)
+        def _(block):
+            @pl.when(block + 1 < total)
+            def _():
+                start_all(1, block + 1)
+
+            wait_all(1, block)
+            work(size, base, block, 0, tp_even, tp_odd)
+
+            @pl.when(block + 2 < total)
+            def _():
+                start_all(0, block + 2)
+
+            @pl.when(block + 1 < total)
+            def _():
+                wait_all(0, block + 1)
+
+            work(size, base, block, 1, tp_odd, tp_even)
 
     def begin():
         start_all(0, 0)
@@ -223,7 +228,7 @@
     cs = math.gcd(local_c, TILE, 8)
     assert cs % 2 == 0 and local_c * NV == cd_local and occupied == virtual and LANES % virtual == 0
     steps = local_c // cs
-    assert steps * (NV // LANES) % 2 == 0
+    assert steps * (NV // LANES) >= 4
     tiles = virtual * virtual // LANES
     place = jnp.stack([first_c, occ_at, vir_at] + [0 * occ_at] * 5)
     facts = jnp.concatenate([place, occ_irrep, vir_tile_irrep]).astype(jnp.int32)
@@ -242,8 +247,8 @@
             in_specs=[pl.BlockSpec(memory_space=pltpu.VMEM)] + [pl.BlockSpec(memory_space=pl.ANY)] * 2,
             out_specs=(pl.BlockSpec(memory_space=pltpu.VMEM),) * 4,
             scratch_shapes=[
-                pltpu.VMEM((2, cs, occupied, occupied, LANES), jnp.bfloat16),
-                pltpu.VMEM((2, cs, virtual, virtual, LANES), jnp.bfloat16),
+                pltpu.VMEM((2, cs, occupied, occupied, 2 * LANES), jnp.bfloat16),
+                pltpu.VMEM((2, cs, virtual, virtual, 2 * LANES), jnp.bfloat16),
                 pltpu.VMEM((IRREPS, tiles, slots * occupied, LANES), jnp.float32),
                 pltpu.VMEM((2, cs // 2, CHUNK * occupied, LANES), jnp.bfloat16),
                 pltpu.VMEM((2, cs // 2, CHUNK * occupied, LANES), jnp.bfloat16),
@@ -256,7 +261,7 @@
                 pltpu.SemaphoreType.DMA((2, 2, cs)),
             ],
         ),
-        compiler_params=pltpu.CompilerParams(vmem_limit_bytes=42 * 1024 * 1024),
+        compiler_params=pltpu.CompilerParams(vmem_limit_bytes=49 * 1024 * 1024),
     )(facts, ycode, amplitudes, ladder_integrals)
 
 

time: 90.5 us -> 82.9 us (0.916); the launches traced: 90.3 us -> 84.4 us
  Pallas kernels: 47.2 us -> 41.3 us
    pallas_call x1, Pallas kernels: 47.2 us -> 41.3 us  [ladder(): pl.pallas_call(functools.partial(ladder_kernel, cs=cs, occ_local=occ_loca...]
where the time goes in v2:
time: 82.9 us; the launch traced here: 84.4 us
  Pallas kernels  41.3 us (50%)
  waiting for transfers between devices  26.3 us (32%)
  starting transfers between devices  12.9 us (16%)
  local copies, waits for them, and re-layouts  3 us (4%)
    pallas_call x1, Pallas kernels, ladder(): pl.pallas_call(functools.partial(ladder_kernel, cs=cs, occ_local=occ_loca...  41.3 us
    ppermute x9, waiting for transfers between devices, swap(): return lax.ppermute(values, axis, [(n, n ^ bit) for n in range(size)])  26.3 us
    ppermute x9, starting transfers between devices, swap(): return lax.ppermute(values, axis, [(n, n ^ bit) for n in range(size)])  12.9 us
  transfers between devices with their start and end apart: 9, of which 6 were waited for; matrix products, arithmetic and copies ran while one was open for 1% of the time, Pallas kernels for 0%

profile of v2, /device:TPU:0, one launch (start us, length us, event | category | flops | bytes accessed | tf_op | source)
XLA Modules:
  0.0 84.4 jit_solution(16963541332288401962)
XLA Ops:
  0.0 0.7 concatenate.3.facts
  0.7 0.7 broadcast_in_dim.2.ycode_ref
  1.5 0.0 copy-start.2
  1.5 0.0 copy-start
  1.5 0.0 copy-start.1
  1.5 41.3 %shard_map.73 = (f32[4,4,128,128]{3,2,1,0:T(8,128)S(1)}, f32[4,4,128,128]{3,2,1,0:T(8,128)S(1)}, f32[4,4,128,128]{3,2,1,0:T(8,128)S(1)}, f32[4,4,128,128]{3,2,1,0:T(8,128)S(1)}) custom-call(s32[52]{0:T(128)S(1)} %concatenate.3.facts, s32[32,128]{1,0:T(8,128)S(1)} %broadcast_in_dim.2.ycode_ref, bf16[32,32,18432]{2,1,0:T(8,128)(2,1)} %t_hbm.1, ...), custom_call_target="tpu_custom_call" | custom-call | tf_op jit(solution)/shard_map/pallas_call | solution.py:241
  42.8 0.5 collective-permute-start.3
  43.3 0.1 collective-permute-start
  43.4 2.2 %collective-permute-done.3 = f32[4,4,128,128]{3,2,1,0:T(8,128)S(1)} collective-permute-done((f32[4,4,128,128]{3,2,1,0:T(8,128)S(1)}, f32[4,4,128,128]{3,2,1,0:T(8,128)S(1)}, u32[]{:S(2)}, u32[]{:S(2)}) %collective-permute-start.3) | collective-permute-done | bytes 1048608 | tf_op jit(solution)/shard_map/ppermute | solution.py:270
  45.6 0.1 slice_add_fusion
  45.8 3.0 %collective-permute-start.4 = (f32[2,4,128,128]{3,2,1,0:T(8,128)S(1)}, f32[2,4,128,128]{3,2,1,0:T(8,128)S(1)}, u32[]{:S(2)}, u32[]{:S(2)}) collective-permute-start(f32[2,4,128,128]{3,2,1,0:T(8,128)S(1)} %get-tuple-element.26), channel_id=1, source_target_pairs={{0,16},{8,24},{16,0},{24,8},{1,17},{9,25},{17,1},{25,9},{2,18},{10... | collective-permute-start | bytes 1572872 | tf_op jit(solution)/shard_map/ppermute | solution.py:270
  48.7 0.0 collective-permute-done
  48.7 0.1 slice_add_fusion.2
  48.8 1.6 %collective-permute-start.1 = (f32[2,4,128,128]{3,2,1,0:T(8,128)S(1)}, f32[2,4,128,128]{3,2,1,0:T(8,128)S(1)}, u32[]{:S(2)}, u32[]{:S(2)}) collective-permute-start(f32[2,4,128,128]{3,2,1,0:T(8,128)S(1)} %get-tuple-element.20), channel_id=1, source_target_pairs={{0,8},{8,0},{16,24},{24,16},{1,9},{9,1},{17,25},{25,17},{2,10},{10... | collective-permute-start | bytes 1572872 | tf_op jit(solution)/shard_map/ppermute | solution.py:270
  50.4 0.0 copy-done.2
  50.4 0.1 dynamic_slice.6
  50.5 10.5 %collective-permute-done.4 = f32[2,4,128,128]{3,2,1,0:T(8,128)S(1)} collective-permute-done((f32[2,4,128,128]{3,2,1,0:T(8,128)S(1)}, f32[2,4,128,128]{3,2,1,0:T(8,128)S(1)}, u32[]{:S(2)}, u32[]{:S(2)}) %collective-permute-start.4) | collective-permute-done | bytes 524320 | tf_op jit(solution)/shard_map/ppermute | solution.py:270
  60.9 0.1 fusion.1
  61.0 1.8 %collective-permute-start.5 = (f32[4,128,128]{2,1,0:T(8,128)S(1)}, f32[4,128,128]{2,1,0:T(8,128)S(1)}, u32[]{:S(2)}, u32[]{:S(2)}) collective-permute-start(f32[4,128,128]{2,1,0:T(8,128)S(1)} %get-tuple-element.28), channel_id=1, source_target_pairs={{0,8},{8,0},{16,24},{24,16},{1,9},{9,1},{17,25},{25,17},{2,10},{10... | collective-permute-start | bytes 786440 | tf_op jit(solution)/shard_map/ppermute | solution.py:270
  62.7 0.0 collective-permute-done.1
  62.7 0.1 fusion.3
  62.8 1.6 %collective-permute-start.2 = (f32[4,128,128]{2,1,0:T(8,128)S(1)}, f32[4,128,128]{2,1,0:T(8,128)S(1)}, u32[]{:S(2)}, u32[]{:S(2)}) collective-permute-start(f32[4,128,128]{2,1,0:T(8,128)S(1)} %get-tuple-element.22), channel_id=1, source_target_pairs={{0,16},{8,24},{16,0},{24,8},{1,17},{9,25},{17,1},{25,9},{2,18},{10... | collective-permute-start | bytes 786440 | tf_op jit(solution)/shard_map/ppermute | solution.py:270
  64.4 0.1 broadcast_add_fusion
  64.5 0.0 copy-done
  64.5 0.2 reshape.53
  64.7 0.0 copy-done.1
  64.7 0.1 dynamic_slice.7
  64.8 4.1 %collective-permute-done.5 = f32[4,128,128]{2,1,0:T(8,128)S(1)} collective-permute-done((f32[4,128,128]{2,1,0:T(8,128)S(1)}, f32[4,128,128]{2,1,0:T(8,128)S(1)}, u32[]{:S(2)}, u32[]{:S(2)}) %collective-permute-start.5) | collective-permute-done | bytes 262176 | tf_op jit(solution)/shard_map/ppermute | solution.py:270
  68.9 1.2 %collective-permute-done.2 = f32[4,128,128]{2,1,0:T(8,128)S(1)} collective-permute-done((f32[4,128,128]{2,1,0:T(8,128)S(1)}, f32[4,128,128]{2,1,0:T(8,128)S(1)}, u32[]{:S(2)}, u32[]{:S(2)}) %collective-permute-start.2) | collective-permute-done | bytes 262176 | tf_op jit(solution)/shard_map/ppermute | solution.py:270
  70.2 1.7 %collective-permute-start.6 = (f32[2,128,128]{2,1,0:T(8,128)S(1)}, f32[2,128,128]{2,1,0:T(8,128)S(1)}, u32[]{:S(2)}, u32[]{:S(2)}) collective-permute-start(f32[2,128,128]{2,1,0:T(8,128)S(1)} %get-tuple-element.37), channel_id=1, source_target_pairs={{0,2},{1,3},{2,0},{3,1},{4,6},{5,7},{6,4},{7,5},{8,10},{9,11},{10,... | collective-permute-start | bytes 393224 | tf_op jit(solution)/shard_map/ppermute | solution.py:270
  71.8 2.6 %collective-permute-start.7 = (f32[2,128,128]{2,1,0:T(8,128)S(1)}, f32[2,128,128]{2,1,0:T(8,128)S(1)}, u32[]{:S(2)}, u32[]{:S(2)}) collective-permute-start(f32[2,128,128]{2,1,0:T(8,128)S(1)} %get-tuple-element.39), channel_id=1, source_target_pairs={{0,4},{1,5},{2,6},{3,7},{4,0},{5,1},{6,2},{7,3},{8,12},{9,13},{10,... | collective-permute-start | bytes 393224 | tf_op jit(solution)/shard_map/ppermute | solution.py:270
  74.4 0.2 collective-permute-start.8
  74.6 0.1 broadcast_subtract_fusion
  74.7 1.2 %collective-permute-done.6 = f32[2,128,128]{2,1,0:T(8,128)S(1)} collective-permute-done((f32[2,128,128]{2,1,0:T(8,128)S(1)}, f32[2,128,128]{2,1,0:T(8,128)S(1)}, u32[]{:S(2)}, u32[]{:S(2)}) %collective-permute-start.6) | collective-permute-done | bytes 131104 | tf_op jit(solution)/shard_map/ppermute | solution.py:270
  75.9 7.1 %collective-permute-done.7 = f32[2,128,128]{2,1,0:T(8,128)S(1)} collective-permute-done((f32[2,128,128]{2,1,0:T(8,128)S(1)}, f32[2,128,128]{2,1,0:T(8,128)S(1)}, u32[]{:S(2)}, u32[]{:S(2)}) %collective-permute-start.7) | collective-permute-done | bytes 131104 | tf_op jit(solution)/shard_map/ppermute | solution.py:270
  83.0 0.0 collective-permute-done.8
  83.0 0.3 reshape.54
  83.3 0.2 fusion
  83.5 0.9 %reshape.55 = f32[8,4,1024]{2,1,0:T(4,128)} reshape(f32[8,4,32,32]{3,2,1,0:T(8,128)S(1)} %fusion) | data formatting | bytes 262144 | tf_op jit(solution)/shard_map/reshape | solution.py:330
  (5 shorter events, 0.1 us)
Async XLA Ops:
  1.5 48.9 %copy-start.2 = (f32[32]{0:T(128)S(1)}, f32[32]{0:T(128)}, u32[]{:S(2)}) copy-start(f32[32]{0:T(128)} %param.10) | copy-start | bytes 388
  1.5 63.0 %copy-start = (f32[8,4,1024]{2,1,0:T(4,128)S(1)}, f32[8,4,1024]{2,1,0:T(4,128)}, u32[]{:S(2)}) copy-start(f32[8,4,1024]{2,1,0:T(4,128)} %param.9) | copy-start | bytes 393220
  1.5 63.2 %copy-start.1 = (f32[32]{0:T(128)S(1)}, f32[32]{0:T(128)}, u32[]{:S(2)}) copy-start(f32[32]{0:T(128)} %param.11) | copy-start | bytes 388
  42.8 2.8 %collective-permute-start.3 = (f32[4,4,128,128]{3,2,1,0:T(8,128)S(1)}, f32[4,4,128,128]{3,2,1,0:T(8,128)S(1)}, u32[]{:S(2)}, u32[]{:S(2)}) collective-permute-start(f32[4,4,128,128]{3,2,1,0:T(8,128)S(1)} %get-tuple-element.24), channel_id=1, source_target_pairs={{0,1},{1,0},{2,3},{3,2},{4,5},{5,4},{6,7},{7,6},{8,9},{9,8},{10,11... | collective-permute-start | bytes 3145736 | tf_op jit(solution)/shard_map/ppermute | solution.py:270
  43.3 5.4 %collective-permute-start = (f32[4,4,128,128]{3,2,1,0:T(8,128)S(1)}, f32[4,4,128,128]{3,2,1,0:T(8,128)S(1)}, u32[]{:S(2)}, u32[]{:S(2)}) collective-permute-start(f32[4,4,128,128]{3,2,1,0:T(8,128)S(1)} %get-tuple-element.18), channel_id=1, source_target_pairs={{0,1},{1,0},{2,3},{3,2},{4,5},{5,4},{6,7},{7,6},{8,9},{9,8},{10,11... | collective-permute-start | bytes 3145736 | tf_op jit(solution)/shard_map/ppermute | solution.py:270
  45.8 15.2 %collective-permute-start.4 = (f32[2,4,128,128]{3,2,1,0:T(8,128)S(1)}, f32[2,4,128,128]{3,2,1,0:T(8,128)S(1)}, u32[]{:S(2)}, u32[]{:S(2)}) collective-permute-start(f32[2,4,128,128]{3,2,1,0:T(8,128)S(1)} %get-tuple-element.26), channel_id=1, source_target_pairs={{0,16},{8,24},{16,0},{24,8},{1,17},{9,25},{17,1},{25,9},{2,18},{10... | collective-permute-start | bytes 1572872 | tf_op jit(solution)/shard_map/ppermute | solution.py:270
  48.8 13.9 %collective-permute-start.1 = (f32[2,4,128,128]{3,2,1,0:T(8,128)S(1)}, f32[2,4,128,128]{3,2,1,0:T(8,128)S(1)}, u32[]{:S(2)}, u32[]{:S(2)}) collective-permute-start(f32[2,4,128,128]{3,2,1,0:T(8,128)S(1)} %get-tuple-element.20), channel_id=1, source_target_pairs={{0,8},{8,0},{16,24},{24,16},{1,9},{9,1},{17,25},{25,17},{2,10},{10... | collective-permute-start | bytes 1572872 | tf_op jit(solution)/shard_map/ppermute | solution.py:270
  61.0 7.9 %collective-permute-start.5 = (f32[4,128,128]{2,1,0:T(8,128)S(1)}, f32[4,128,128]{2,1,0:T(8,128)S(1)}, u32[]{:S(2)}, u32[]{:S(2)}) collective-permute-start(f32[4,128,128]{2,1,0:T(8,128)S(1)} %get-tuple-element.28), channel_id=1, source_target_pairs={{0,8},{8,0},{16,24},{24,16},{1,9},{9,1},{17,25},{25,17},{2,10},{10... | collective-permute-start | bytes 786440 | tf_op jit(solution)/shard_map/ppermute | solution.py:270
  62.8 7.3 %collective-permute-start.2 = (f32[4,128,128]{2,1,0:T(8,128)S(1)}, f32[4,128,128]{2,1,0:T(8,128)S(1)}, u32[]{:S(2)}, u32[]{:S(2)}) collective-permute-start(f32[4,128,128]{2,1,0:T(8,128)S(1)} %get-tuple-element.22), channel_id=1, source_target_pairs={{0,16},{8,24},{16,0},{24,8},{1,17},{9,25},{17,1},{25,9},{2,18},{10... | collective-permute-start | bytes 786440 | tf_op jit(solution)/shard_map/ppermute | solution.py:270
  70.2 5.7 %collective-permute-start.6 = (f32[2,128,128]{2,1,0:T(8,128)S(1)}, f32[2,128,128]{2,1,0:T(8,128)S(1)}, u32[]{:S(2)}, u32[]{:S(2)}) collective-permute-start(f32[2,128,128]{2,1,0:T(8,128)S(1)} %get-tuple-element.37), channel_id=1, source_target_pairs={{0,2},{1,3},{2,0},{3,1},{4,6},{5,7},{6,4},{7,5},{8,10},{9,11},{10,... | collective-permute-start | bytes 393224 | tf_op jit(solution)/shard_map/ppermute | solution.py:270
  71.8 11.2 %collective-permute-start.7 = (f32[2,128,128]{2,1,0:T(8,128)S(1)}, f32[2,128,128]{2,1,0:T(8,128)S(1)}, u32[]{:S(2)}, u32[]{:S(2)}) collective-permute-start(f32[2,128,128]{2,1,0:T(8,128)S(1)} %get-tuple-element.39), channel_id=1, source_target_pairs={{0,4},{1,5},{2,6},{3,7},{4,0},{5,1},{6,2},{7,3},{8,12},{9,13},{10,... | collective-permute-start | bytes 393224 | tf_op jit(solution)/shard_map/ppermute | solution.py:270
  74.4 8.6 %collective-permute-start.8 = (f32[2,128,128]{2,1,0:T(8,128)S(1)}, f32[2,128,128]{2,1,0:T(8,128)S(1)}, u32[]{:S(2)}, u32[]{:S(2)}) collective-permute-start(f32[2,128,128]{2,1,0:T(8,128)S(1)} %get-tuple-element.38), channel_id=1, source_target_pairs={{0,6},{1,7},{2,4},{3,5},{4,2},{5,3},{6,0},{7,1},{8,14},{9,15},{10,... | collective-permute-start | bytes 393224 | tf_op jit(solution)/shard_map/ppermute | solution.py:270
